TPU v7x, 32 devices: a whole 2x2x4 slice. The times are simulated.
32 devices in a mesh: band: 8 (over y, x, core), grid: 4 (over z).
Axes of the slice: x: 2, y: 2, z: 4, core: 2. Of those that a mesh axis runs over, the one named last changes fastest.
Arguments:
- valence: bfloat16 [16, 2, 160, 160, 160], P('band', None, 'grid'), may hold values from -6 to 6
- conduction: bfloat16 [8, 2, 160, 160, 160], P('band', None, 'grid'), may hold values from -6 to 6
- val_energy: float32 [16], replicated, may hold values from -12 to -1
- cond_energy: float32 [8], replicated, may hold values from 1 to 16
- cond_band: int32 [8], P('band'), may hold values from 0 to 7, each once
- owners: int32 [2], replicated, may hold values from 0 to 7
- gvectors: int32 [3, 4096], replicated, may hold values from 0 to 159, as said below
Outputs:
- chi0: float32 [2, 4096, 4096], P(None, 'grid', 'band')
Inputs may be any that keep to these rules, and one draw needn't show every extreme that they name: `gvectors`: the G-vectors are distinct; each component, read between -80 and 80, lies within -10 to 10. `owners`: each entry is an index along band. `cond_band`: A permutation of the global conduction band numbers.
All inputs are finite; a program needn't handle non-finite values.
Results may differ from a plain program's by a relative error of at most 0.0092.
Values may be sent and summed in bfloat16 or wider, within the bound.
A program may use at most 192 MiB of HBM per device.

v0:
```python
import math

import jax
import jax.numpy as jnp
from jax import lax
from jax.sharding import PartitionSpec as P

ROUNDS = 2


def from_root(block, axis, owner):
    block = jnp.where(lax.axis_index(axis) == owner, block, jnp.zeros_like(block))
    return lax.psum(block, axis)


def dft_tables(length):
    positions = jnp.arange(length, dtype=jnp.int32)
    phase_index = positions[:, None] * positions[None, :] % length
    angles = phase_index.astype(jnp.float32) * (2.0 * math.pi / length)
    return (jnp.cos(angles).astype(jnp.bfloat16), jnp.sin(angles).astype(jnp.bfloat16))


def wide_table(cos_table, sin_table):
    top_half = jnp.concatenate([cos_table, -sin_table], axis=1)
    low_half = jnp.concatenate([sin_table, cos_table], axis=1)
    return jnp.concatenate([top_half, low_half], axis=0)


def plane_transform(density, wide, cos_table, sin_table):
    length = cos_table.shape[0]
    along_z = jnp.einsum("bxyk,kq->bxyq", density, wide, preferred_element_type=jnp.float32).astype(
        jnp.bfloat16
    )
    cos_part = jnp.einsum("bxyk,yq->bxqk", along_z, cos_table, preferred_element_type=jnp.float32)
    sin_part = jnp.einsum("bxyk,yq->bxqk", along_z, sin_table, preferred_element_type=jnp.float32)
    real_part = cos_part[..., :length] + sin_part[..., length:]
    imag_part = cos_part[..., length:] - sin_part[..., :length]
    return jnp.concatenate([real_part, imag_part], axis=-1).astype(jnp.bfloat16)


def shards(valence, conduction, val_energy, cond_energy, cond_band, owners, gvectors):
    val_dev = valence.shape[0]
    cond_dev = conduction.shape[0]
    x_local = valence.shape[2]
    length = valence.shape[3]
    y_local = length // lax.axis_size("grid")
    grid_pos = lax.axis_index("grid")
    band_pos = lax.axis_index("band")
    cos_table, sin_table = dft_tables(length)
    wide = wide_table(cos_table, sin_table)
    freq_x, freq_y, freq_z = (gvectors[0], gvectors[1], gvectors[2])
    norm_factor = float(length) ** (-1.5)
    pairs_all = ROUNDS * val_dev * cond_dev * lax.axis_size("band")
    cond_numbers = jnp.arange(cond_energy.shape[0], dtype=jnp.int32)
    cond_levels = jnp.sum(
        jnp.where(cond_band[:, None] == cond_numbers[None, :], cond_energy[None, :], 0.0), axis=1
    )
    cond_f = conduction.astype(jnp.float32)[None]
    local_y = freq_y - grid_pos * y_local
    inside = (local_y >= 0) & (local_y < y_local)
    local_y = jnp.clip(local_y, 0, y_local - 1)
    elem_rounds = []
    weight_rounds = []
    for round_no in range(ROUNDS):
        owner_pos = owners[round_no]
        val_bands = from_root(valence, "band", owner_pos)
        val_levels = lax.dynamic_slice_in_dim(val_energy, owner_pos * val_dev, val_dev, 0)
        val_f = val_bands.astype(jnp.float32)[:, None]
        dens_re = val_f[:, :, 0] * cond_f[:, :, 0] + val_f[:, :, 1] * cond_f[:, :, 1]
        dens_im = val_f[:, :, 0] * cond_f[:, :, 1] - val_f[:, :, 1] * cond_f[:, :, 0]
        density = jnp.concatenate([dens_re, dens_im], axis=-1).astype(jnp.bfloat16)
        density = density.reshape(val_dev * cond_dev, x_local, length, 2 * length)
        plane = plane_transform(density, wide, cos_table, sin_table)
        block = lax.all_to_all(plane, "grid", split_axis=2, concat_axis=1, tiled=True)
        cos_part = jnp.einsum("bxyk,xq->bqyk", block, cos_table, preferred_element_type=jnp.float32)
        sin_part = jnp.einsum("bxyk,xq->bqyk", block, sin_table, preferred_element_type=jnp.float32)
        full_re = cos_part[..., :length] + sin_part[..., length:]
        full_im = cos_part[..., length:] - sin_part[..., :length]
        elem_re = jnp.where(inside[None, :], full_re[:, freq_x, local_y, freq_z], 0.0) * norm_factor
        elem_im = jnp.where(inside[None, :], full_im[:, freq_x, local_y, freq_z], 0.0) * norm_factor
        elem_round = jnp.stack([elem_re, elem_im], axis=1)
        elem_rounds.append(elem_round)
        pair_weight = 2.0 / (pairs_all * (val_levels[:, None] - cond_levels[None, :]))
        weight_rounds.append(pair_weight.reshape(val_dev * cond_dev))
    local_elements = jnp.concatenate(elem_rounds, axis=0)
    local_weights = jnp.concatenate(weight_rounds, axis=0)
    summed = lax.psum(local_elements, "grid")
    row_count = summed.shape[2] // lax.axis_size("grid")
    col_count = summed.shape[2] // lax.axis_size("band")
    gathered, all_weights = (
        lax.all_gather(summed, "band", axis=0, tiled=True),
        lax.all_gather(local_weights, "band", axis=0, tiled=True),
    )
    row_block = lax.dynamic_slice_in_dim(gathered, grid_pos * row_count, row_count, 2)
    col_block = lax.dynamic_slice_in_dim(gathered, band_pos * col_count, col_count, 2)
    weighted = row_block * all_weights[:, None, None]
    right_side = jnp.concatenate([col_block[:, 0], col_block[:, 1]], axis=0)
    left_real = jnp.concatenate([weighted[:, 0], weighted[:, 1]], axis=0)
    left_imag = jnp.concatenate([weighted[:, 1], -weighted[:, 0]], axis=0)
    high = lax.Precision.HIGHEST
    chi_re = jnp.einsum("pr,pc->rc", left_real, right_side, precision=high)
    chi_im = jnp.einsum("pr,pc->rc", left_imag, right_side, precision=high)
    return jnp.stack([chi_re, chi_im])


def solution(mesh):
    return jax.shard_map(
        shards,
        mesh=mesh,
        in_specs=(
            P("band", None, "grid", None, None),
            P("band", None, "grid", None, None),
            P(),
            P(),
            P("band"),
            P(),
            P(),
        ),
        out_specs=P(None, "grid", "band"),
        check_vma=False,
    )
```

profile of v0, /device:TPU:0, one launch (start us, length us, event | category | flops | bytes accessed | tf_op | source)
XLA Modules:
  0.0 1374.8 jit_solution(3738130654744422996)
XLA Ops:
  9.1 14.2 %select_bitcast_fusion.1 = (bf16[2,1,2,40,160,160]{5,4,3,0,2,1:T(8,128)(2,1)}, bf16[2,1,2,40,160,160]{5,4,3,0,2,1:T(8,128)(2,1)}) fusion(pred[]{:T(512)S(6)} %eq.19, bf16[2,2,40,160,160]{4,3,2,1,0:T(8,128)(2,1)} %param.7, pred[]{:T(512)S(6)} %eq.20), kind=kLoop, calls=%fused_computation.25 | loop fusion | flops 8192000 | bytes 24576002 | tf_op jit(solution)/shard_map/broadcast_in_dim | solution.py:68
  24.6 10.3 bitcast_convert_fusion
  34.9 11.4 slice_bitcast_fusion.5
  46.2 299.0 %all-reduce.7.cloned.1.call-done = (bf16[2,1,2,40,160,160]{5,4,3,0,2,1:T(8,128)(2,1)}, bf16[2,1,2,40,160,160]{5,4,3,0,2,1:T(8,128)(2,1)}) async-done(((bf16[2,1,2,40,160,160]{5,4,3,0,2,1:T(8,128)(2,1)}, bf16[2,1,2,40,160,160]{5,4,3,0,2,1:T(8,128)(2,1)}), (bf16[2,1,2,40,160,160]{5,4,3,0,2,1:T(8,128)(2,1)}, bf16[2,1,2,40,160,160]{5,4,3,0,2,1:T(8,128)(2,1)})) %all-reduce.7.cloned.1.call-update) | async-done | bytes 16384016 | tf_op jit(solution)/shard_map/psum | solution.py:13
  345.2 15.7 %broadcast_in_dim.74 = f32[2,1,2,40,160,160]{5,4,3,0,2,1:T(8,128)} convert(bf16[2,1,2,40,160,160]{5,4,3,0,2,1:T(8,128)(2,1)} %get-tuple-element.6) | non-fusion elementwise | flops 4096000 | bytes 24576000 | tf_op jit(solution)/shard_map/broadcast_in_dim | solution.py:68
  372.6 32.0 %add_convert_fusion.1 = (bf16[2,40,160,160]{3,2,1,0:T(8,128)(2,1)}, bf16[2,40,160,160]{3,2,1,0:T(8,128)(2,1)}, bf16[2,40,160,160]{3,2,1,0:T(8,128)(2,1)}, bf16[2,40,160,160]{3,2,1,0:T(8,128)(2,1)}) fusion(f32[2,1,2,40,160,160]{5,4,3,0,2,1:T(8,128)} %broadcast_in_dim.74, f32[40,160,160]{2,1,0:T(8,128)} %get-tuple-element.22, ...), kind=kLoop, calls=%fused_computation.24 | loop fusion | flops 32768000 | bytes 57344000 | tf_op jit(solution)/shard_map/convert.9
  404.6 12.0 fusion.12
  423.4 13.8 %convolution_bitcast_fusion.3 = f32[2,40,160,320]{3,2,1,0:T(8,128)} fusion(bf16[2,40,160,320]{3,2,1,0:T(8,128)(2,1)} %fusion.12), kind=kOutput, calls=%fused_computation.39 | convolution fusion | flops 1310976000 | bytes 24576000 | tf_op jit(solution)/shard_map/bxyk,yq->bxqk/dot_general | solution.py:34
  437.2 16.1 %fusion.1 = (bf16[2,40,160,160]{3,2,1,0:T(8,128)(2,1)}, bf16[2,40,160,160]{3,2,1,0:T(8,128)(2,1)}) fusion(f32[2,40,160,320]{3,2,1,0:T(8,128)S(1)} %convolution_bitcast_fusion.2, f32[2,40,160,320]{3,2,1,0:T(8,128)} %convolution_bitcast_fusion.3), kind=kLoop, calls=%fused_computation.9 | loop fusion | flops 8192000 | bytes 40960000 | tf_op jit(solution)/shard_map/convert.3
  453.3 12.3 pad_maximum_fusion.1
  465.6 11.1 copy.52
  482.9 12.0 fusion.15
  501.5 13.8 %convolution_bitcast_fusion.7 = f32[2,40,160,320]{3,2,1,0:T(8,128)} fusion(bf16[2,40,160,320]{3,2,1,0:T(8,128)(2,1)} %fusion.15), kind=kOutput, calls=%fused_computation.43 | convolution fusion | flops 1310976000 | bytes 24576000 | tf_op jit(solution)/shard_map/bxyk,yq->bxqk/dot_general | solution.py:34
  515.3 16.0 %fusion.3 = (bf16[2,40,160,160]{3,2,1,0:T(8,128)(2,1)}, bf16[2,40,160,160]{3,2,1,0:T(8,128)(2,1)}) fusion(f32[2,40,160,320]{3,2,1,0:T(8,128)S(1)} %convolution_bitcast_fusion.6, f32[2,40,160,320]{3,2,1,0:T(8,128)} %convolution_bitcast_fusion.7), kind=kLoop, calls=%fused_computation.17 | loop fusion | flops 8192000 | bytes 40960000 | tf_op jit(solution)/shard_map/convert.7
  531.3 12.7 pad_maximum_fusion
  543.9 11.2 copy.43
  555.1 141.9 %all-to-all-done.1 = bf16[2,40,160,320]{3,1,0,2:T(8,128)(2,1)} async-done(((bf16[2,40,160,320]{3,1,0,2:T(8,128)(2,1)}), bf16[2,40,160,320]{3,1,0,2:T(8,128)(2,1)}, u32[]{:S(2)}, u32[]{:S(2)}) %all-to-all-start.1) | async-done | bytes 8192032 | tf_op jit(solution)/shard_map/all_to_all | solution.py:74
  711.7 13.9 %convolution_bitcast_fusion = f32[2,160,40,320]{3,1,2,0:T(8,128)} fusion(bf16[2,160,40,320]{3,1,2,0:T(8,128)(2,1)} %bitcast.155), kind=kOutput, calls=%fused_computation.36 | convolution fusion | flops 1310976000 | bytes 24576000 | tf_op jit(solution)/shard_map/bxyk,xq->bqyk/dot_general | solution.py:76
  734.6 181.8 %all-to-all-done = bf16[2,40,160,320]{3,1,0,2:T(8,128)(2,1)} async-done(((bf16[2,40,160,320]{3,1,0,2:T(8,128)(2,1)}), bf16[2,40,160,320]{3,1,0,2:T(8,128)(2,1)}, u32[]{:S(2)}, u32[]{:S(2)}) %all-to-all-start) | async-done | bytes 8192032 | tf_op jit(solution)/shard_map/all_to_all | solution.py:74
  924.9 14.0 %convolution_bitcast_fusion.4 = f32[2,160,40,320]{3,1,2,0:T(8,128)} fusion(bf16[2,160,40,320]{3,1,2,0:T(8,128)(2,1)} %bitcast.157), kind=kOutput, calls=%fused_computation.40 | convolution fusion | flops 1310976000 | bytes 24576000 | tf_op jit(solution)/shard_map/bxyk,xq->bqyk/dot_general | solution.py:76
  947.6 23.1 %slice_add_fusion = (f32[2,160,40,160]{3,1,2,0:T(8,128)S(1)}, f32[2,160,40,160]{3,1,2,0:T(8,128)}) fusion(f32[2,160,40,320]{3,1,2,0:T(8,128)} %convolution_bitcast_fusion, f32[2,160,40,320]{3,1,2,0:T(8,128)} %convolution_bitcast_fusion.1), kind=kLoop, calls=%fused_computation.5 | loop fusion | flops 4096000 | bytes 49152000 | tf_op jit(solution)/shard_map/add | solution.py:77
  970.8 27.5 %copy.57 = f32[2,160,40,160]{3,0,2,1:T(2,128)} copy(f32[2,160,40,160]{3,1,2,0:T(8,128)} %get-tuple-element.14) | data formatting | bytes 16384000 | tf_op jit(solution)/shard_map/sub | solution.py:78
  998.3 22.8 %copy.56 = f32[2,160,40,160]{3,0,2,1:T(2,128)} copy(f32[2,160,40,160]{3,1,2,0:T(8,128)S(1)} %get-tuple-element.13) | data formatting | bytes 16384000 | tf_op jit(solution)/shard_map/add | solution.py:77
  1021.1 51.5 %gather_fusion.3 = f32[4096,2]{0,1:T(2,128)S(1)} fusion(f32[2,160,40,160]{3,0,2,1:T(2,128)} %copy.57, s32[4096]{0:T(1024)S(1)} %bitcast.151), kind=kCustom, calls=%fused_computation.3 | custom fusion | bytes 114688 | tf_op jit(solution)/shard_map/gather | solution.py:80
  1072.5 51.3 %gather_fusion.2 = f32[4096,2]{0,1:T(2,128)S(1)} fusion(f32[2,160,40,160]{3,0,2,1:T(2,128)} %copy.56, s32[4096]{0:T(1024)S(1)} %bitcast.152), kind=kCustom, calls=%fused_computation.2 | custom fusion | bytes 114688 | tf_op jit(solution)/shard_map/gather | solution.py:79
  1123.8 23.2 %slice_add_fusion.2 = (f32[2,160,40,160]{3,1,2,0:T(8,128)}, f32[2,160,40,160]{3,1,2,0:T(8,128)S(1)}) fusion(f32[2,160,40,320]{3,1,2,0:T(8,128)} %convolution_bitcast_fusion.4, f32[2,160,40,320]{3,1,2,0:T(8,128)} %convolution_bitcast_fusion.5), kind=kLoop, calls=%fused_computation.13 | loop fusion | flops 4096000 | bytes 49152000 | tf_op jit(solution)/shard_map/add | solution.py:77
  1147.0 22.8 %copy.48 = f32[2,160,40,160]{3,0,2,1:T(2,128)} copy(f32[2,160,40,160]{3,1,2,0:T(8,128)S(1)} %get-tuple-element.8) | data formatting | bytes 16384000 | tf_op jit(solution)/shard_map/sub | solution.py:78
  1169.8 51.4 %gather_fusion.1 = f32[4096,2]{0,1:T(2,128)S(1)} fusion(f32[2,160,40,160]{3,0,2,1:T(2,128)} %copy.48, s32[4096]{0:T(1024)S(1)} %bitcast.153), kind=kCustom, calls=%fused_computation.1 | custom fusion | bytes 114688 | tf_op jit(solution)/shard_map/gather | solution.py:80
  1221.2 27.6 %copy.47 = f32[2,160,40,160]{3,0,2,1:T(2,128)} copy(f32[2,160,40,160]{3,1,2,0:T(8,128)} %get-tuple-element.7) | data formatting | bytes 16384000 | tf_op jit(solution)/shard_map/add | solution.py:77
  1248.8 51.4 %gather_fusion = f32[4096,2]{0,1:T(2,128)S(1)} fusion(f32[2,160,40,160]{3,0,2,1:T(2,128)} %copy.47, s32[4096]{0:T(1024)S(1)} %bitcast.154), kind=kCustom, calls=%fused_computation | custom fusion | bytes 114688 | tf_op jit(solution)/shard_map/gather | solution.py:79
  1301.1 32.7 %all-reduce.5.cloned.1.call-done = f32[4,2,4096]{2,0,1:T(4,128)} async-done(((f32[4,2,4096]{2,0,1:T(4,128)}), f32[4,2,4096]{2,0,1:T(4,128)}) %all-reduce.5.cloned.1.call-update) | async-done | bytes 131088 | tf_op jit(solution)/shard_map/psum | solution.py:87
  1340.0 11.9 all-reduce
  (54 shorter events, 95.2 us)
Async XLA Ops:
  6.5 338.7 %all-reduce.7.cloned.1.call-start = ((), (), s32[]{:S(2)}) async-start(), calls=%async_computation.4 | async-start | bytes 52428800 | tf_op jit(solution)/shard_map/psum | solution.py:13
  345.2 18.1 %copy-start.2 = (bf16[2,1,2,40,160,160]{5,4,3,0,2,1:T(8,128)(2,1)S(1)}, bf16[2,1,2,40,160,160]{5,4,3,0,2,1:T(8,128)(2,1)}, u32[]{:S(2)}) copy-start(bf16[2,1,2,40,160,160]{5,4,3,0,2,1:T(8,128)(2,1)} %get-tuple-element.5) | copy-start | bytes 24576004
  476.7 220.3 %all-to-all-start.1 = ((bf16[2,40,160,320]{3,1,0,2:T(8,128)(2,1)}), bf16[2,40,160,320]{3,1,0,2:T(8,128)(2,1)}, u32[]{:S(2)}, u32[]{:S(2)}) async-start(bf16[2,40,160,320]{3,1,0,2:T(8,128)(2,1)} %copy.52), calls=%async_computation.1 | async-start | bytes 19660800 | tf_op jit(solution)/shard_map/all_to_all | solution.py:74
  555.1 147.8 %copy-start.3 = (s32[3,4096]{1,0:T(4,128)S(1)}, s32[3,4096]{1,0:T(4,128)}, u32[]{:S(2)}) copy-start(s32[3,4096]{1,0:T(4,128)} %param.13) | copy-start | bytes 147460
  697.0 219.3 %all-to-all-start = ((bf16[2,40,160,320]{3,1,0,2:T(8,128)(2,1)}), bf16[2,40,160,320]{3,1,0,2:T(8,128)(2,1)}, u32[]{:S(2)}, u32[]{:S(2)}) async-start(bf16[2,40,160,320]{3,1,0,2:T(8,128)(2,1)} %copy.43), calls=%async_computation | async-start | bytes 19660800 | tf_op jit(solution)/shard_map/all_to_all | solution.py:74
  702.9 630.9 %all-reduce.5.cloned.1.call-start = ((), (), s32[]{:S(2)}) async-start(), calls=%async_computation.2 | async-start | bytes 262144 | tf_op jit(solution)/shard_map/psum | solution.py:87
  711.7 13.9 %copy-start = (bf16[2,40,4,40,320]{4,1,2,3,0:T(8,128)(2,1)S(1)}, bf16[2,40,4,40,320]{4,1,2,3,0:T(8,128)(2,1)}, u32[]{:S(2)}) copy-start(bf16[2,40,4,40,320]{4,1,2,3,0:T(8,128)(2,1)} %copy.53) | copy-start | bytes 24576004
  924.9 14.0 %copy-start.1 = (bf16[2,40,4,40,320]{4,1,2,3,0:T(8,128)(2,1)S(1)}, bf16[2,40,4,40,320]{4,1,2,3,0:T(8,128)(2,1)}, u32[]{:S(2)}) copy-start(bf16[2,40,4,40,320]{4,1,2,3,0:T(8,128)(2,1)} %copy.44) | copy-start | bytes 24576004
  1221.2 116.1 %copy-start.6 = (u32[32]{0:T(128)S(1)}, u32[32]{0:T(128)}, u32[]{:S(2)}) copy-start(u32[32]{0:T(128)} %constant.132) | copy-start | bytes 388
  1221.2 117.4 %copy-start.5 = (f32[8]{0:T(128)S(1)}, f32[8]{0:T(128)}, u32[]{:S(2)}) copy-start(f32[8]{0:T(128)} %param.10) | copy-start | bytes 100
  1221.2 118.0 %copy-start.4 = (f32[16]{0:T(128)S(1)}, f32[16]{0:T(128)}, u32[]{:S(2)}) copy-start(f32[16]{0:T(128)} %param.9) | copy-start | bytes 196
  1301.0 58.0 %all-gather.2.cloned.1.call-start = ((), (), s32[]{:S(2)}) async-start(), calls=%async_computation.3 | async-start | bytes 1179648 | tf_op jit(solution)/shard_map/all_gather | solution.py:91
Sparse Core Ops, SparseCore 0:
  23.4 321.8 all-reduce.6
  1301.1 32.5 all-reduce.4
  1335.8 23.1 all-gather.1
where the time goes:
time: 1390 us; the launch traced here: 1370 us
  waiting for transfers between devices  662 us (48%)
  local copies, waits for them, and re-layouts  365 us (26%)
  other arithmetic  192 us (14%)
  matrix products  114 us (8%)
  between operations  17.5 us (1%)
    all_to_all x2, waiting for transfers between devices, shards(): lax.all_to_all(plane, 'grid', split_axis=2, concat_axis=1, tiled=True)  324 us
    psum x1, waiting for transfers between devices, from_root(): return lax.psum(block, axis)  299 us
    gather x2, local copies, waits for them, and re-layouts, shards(): full_im[:, freq_x, local_y, freq_z]  103 us
    gather x2, local copies, waits for them, and re-layouts, shards(): full_re[:, freq_x, local_y, freq_z]  103 us
    another operation x3, other arithmetic  64.1 us
    add x2, local copies, waits for them, and re-layouts, shards(): full_re = cos_part[..., :length] + sin_part[..., length:]  50.3 us
    sub x2, local copies, waits for them, and re-layouts, shards(): full_im = cos_part[..., length:] - sin_part[..., :length]  50.3 us
    add x2, other arithmetic, shards(): full_re = cos_part[..., :length] + sin_part[..., length:]  46.3 us
  transfers between devices with their start and end apart: 5, of which 5 were waited for; matrix products, arithmetic and copies ran while one was open for 9% of the time, Pallas kernels for 0%

commit v1 on v0

v1 whole, which is shorter than its diff:
```python
import math

import jax
import jax.numpy as jnp
from jax import lax
from jax.sharding import PartitionSpec as P

ROUNDS = 2
GMAX = 10
SIDE = 2 * GMAX + 1


def from_root(block, axis, owner):
    block = jnp.where(lax.axis_index(axis) == owner, block, jnp.zeros_like(block))
    return lax.psum(block, axis)


def twiddles(freqs, positions, length):
    phase = (freqs * positions) % length
    angles = phase.astype(jnp.float32) * (2.0 * math.pi / length)
    return jnp.cos(angles).astype(jnp.bfloat16), jnp.sin(angles).astype(jnp.bfloat16)


def low_tables(length):
    freqs = (jnp.arange(SIDE, dtype=jnp.int32) - GMAX) % length
    return twiddles(freqs[None, :], jnp.arange(length, dtype=jnp.int32)[:, None], length)


def planes_of(valence, conduction, owners):
    length = valence.shape[3]
    val_dev, x_local = valence.shape[0], valence.shape[2]
    cos_low, sin_low = low_tables(length)
    wide = jnp.concatenate(
        [
            jnp.concatenate([cos_low, -sin_low], axis=1),
            jnp.concatenate([sin_low, cos_low], axis=1),
        ],
        axis=0,
    )
    cond_f = conduction[0].astype(jnp.float32)
    planes = []
    for round_no in range(ROUNDS):
        val_bands = from_root(valence, "band", owners[round_no]).astype(jnp.float32)
        dens_re = val_bands[:, 0] * cond_f[0] + val_bands[:, 1] * cond_f[1]
        dens_im = val_bands[:, 0] * cond_f[1] - val_bands[:, 1] * cond_f[0]
        density = jnp.concatenate([dens_re, dens_im], axis=-1).astype(jnp.bfloat16)
        along_z = jnp.einsum(
            "bxyk,kq->bxyq", density, wide, preferred_element_type=jnp.float32
        ).astype(jnp.bfloat16)
        cos_part = jnp.einsum("bxyk,yq->bxqk", along_z, cos_low, preferred_element_type=jnp.float32)
        sin_part = jnp.einsum("bxyk,yq->bxqk", along_z, sin_low, preferred_element_type=jnp.float32)
        real_part = cos_part[..., :SIDE] + sin_part[..., SIDE:]
        imag_part = cos_part[..., SIDE:] - sin_part[..., :SIDE]
        plane = jnp.stack([real_part, imag_part], axis=1).astype(jnp.bfloat16)
        planes.append(plane.reshape(val_dev, 2, x_local, SIDE * SIDE))
    return jnp.concatenate(planes, axis=0)


def chi_block(plane, gvectors, scale, length):
    grid_pos = lax.axis_index("grid")
    band_pos = lax.axis_index("band")
    pairs, _, x_local, _ = plane.shape
    freq_x, freq_y, freq_z = (gvectors[0], gvectors[1], gvectors[2])
    count = freq_x.shape[0]
    column = (freq_y + GMAX) % length * SIDE + (freq_z + GMAX) % length
    chosen = (jnp.arange(SIDE * SIDE, dtype=jnp.int32)[:, None] == column[None, :]).astype(jnp.bfloat16)
    at_g = jnp.dot(
        plane.reshape(pairs * 2 * x_local, SIDE * SIDE), chosen, preferred_element_type=jnp.float32
    ).reshape(pairs, 2, x_local, count)
    positions = grid_pos * x_local + jnp.arange(x_local, dtype=jnp.int32)
    cos_g, sin_g = twiddles(freq_x[None, :], positions[:, None], length)
    cos_g, sin_g = cos_g.astype(jnp.float32), sin_g.astype(jnp.float32)
    elem_re = jnp.sum(at_g[:, 0] * cos_g + at_g[:, 1] * sin_g, axis=1)
    elem_im = jnp.sum(at_g[:, 1] * cos_g - at_g[:, 0] * sin_g, axis=1)
    local = jnp.stack([elem_re, elem_im], axis=1) * scale[:, None, None]
    summed = lax.psum(local, "grid")
    gathered = lax.all_gather(summed, "band", axis=0, tiled=True)
    row_count = count // lax.axis_size("grid")
    col_count = count // lax.axis_size("band")
    rows = lax.dynamic_slice_in_dim(gathered, grid_pos * row_count, row_count, 2)
    cols = lax.dynamic_slice_in_dim(gathered, band_pos * col_count, col_count, 2)
    right_side = jnp.concatenate([cols[:, 0], cols[:, 1]], axis=0)
    left_real = jnp.concatenate([-rows[:, 0], -rows[:, 1]], axis=0)
    left_imag = jnp.concatenate([-rows[:, 1], rows[:, 0]], axis=0)
    high = lax.Precision.HIGHEST
    chi_re = jnp.einsum("pr,pc->rc", left_real, right_side, precision=high)
    chi_im = jnp.einsum("pr,pc->rc", left_imag, right_side, precision=high)
    return jnp.stack([chi_re, chi_im])


def pair_scale(val_energy, cond_energy, cond_band, owners, val_dev, length):
    pairs_all = ROUNDS * val_dev * cond_band.shape[0] * lax.axis_size("band")
    cond_numbers = jnp.arange(cond_energy.shape[0], dtype=jnp.int32)
    cond_level = jnp.sum(jnp.where(cond_band[0] == cond_numbers, cond_energy, 0.0))
    val_numbers = (owners[:, None] * val_dev + jnp.arange(val_dev, dtype=jnp.int32)[None]).reshape(-1)
    which = val_numbers[:, None] == jnp.arange(val_energy.shape[0], dtype=jnp.int32)[None]
    val_levels = jnp.sum(jnp.where(which, val_energy[None], 0.0), axis=1)
    return jnp.sqrt(2.0 / (pairs_all * (cond_level - val_levels))) * float(length) ** (-1.5)


def shards(valence, conduction, val_energy, cond_energy, cond_band, owners, gvectors):
    length = valence.shape[3]
    plane = planes_of(valence, conduction, owners)
    scale = pair_scale(val_energy, cond_energy, cond_band, owners, valence.shape[0], length)
    return chi_block(plane, gvectors, scale, length)


def solution(mesh):
    return jax.shard_map(
        shards,
        mesh=mesh,
        in_specs=(
            P("band", None, "grid", None, None),
            P("band", None, "grid", None, None),
            P(),
            P(),
            P("band"),
            P(),
            P(),
        ),
        out_specs=P(None, "grid", "band"),
        check_vma=False,
    )
```

time: 1390 us -> 514 us (0.37); the launches traced: 1370 us -> 514 us
  local copies, waits for them, and re-layouts: 365 us -> 24.3 us
  waiting for transfers between devices: 662 us -> 354 us
  other arithmetic: 192 us -> 94.8 us
  matrix products: 114 us -> 24.6 us
    all_to_all x2 -> x0, waiting for transfers between devices: 324 us -> none  [shards(): lax.all_to_all(plane, 'grid', split_axis=2, concat_axis=1, tiled=True)]
    gather x4 -> x0, local copies, waits for them, and re-layouts: 206 us -> none  [the longest x2 103 us: shards(): full_im[:, freq_x, local_y, freq_z]]
    dot_general x12 -> x9, matrix products: 114 us -> 24.6 us  [the longest x2 14.5 us: planes_of(): jnp.einsum('bxyk,kq->bxyq', density, wide, preferred_element_type=jnp.flo...]
    sub x2 -> x0, local copies, waits for them, and re-layouts: 50.3 us -> none  [shards(): full_im = cos_part[..., length:] - sin_part[..., :length]]
    add x2 -> x1, local copies, waits for them, and re-layouts: 50.3 us -> 0.08 us  [pair_scale(): owners[:, None] * val_dev + jnp.arange(val_dev, dtype=jnp.int32)[None]]
    broadcast_in_dim x4 -> x0, other arithmetic: 49.3 us -> none  [the longest x3 39 us: shards(): val_f = val_bands.astype(jnp.float32)[:, None]]
    add x2, other arithmetic: 46.3 us -> 0.08 us  [the longest x1 0.07 us: pair_scale(): owners[:, None] * val_dev + jnp.arange(val_dev, dtype=jnp.int32)[None]]
    convert_element_type x1 -> x5, other arithmetic: 0.69 us -> 38 us  [the longest x2 24.8 us: planes_of(): val_bands = from_root(valence, 'band', owners[round_no]).astype(jnp.float32)]
  transfers between devices with their start and end apart: 5 -> 3, of which waited for: 5 -> 3; matrix products, arithmetic and copies ran while one was open for 9% -> 5% of each run, Pallas kernels for 0% -> 0%
where the time goes in v1:
time: 514 us
  waiting for transfers between devices  354 us (69%)
  other arithmetic  94.8 us (18%)
  matrix products  24.6 us (5%)
  local copies, waits for them, and re-layouts  24.3 us (5%)
  between operations  15.3 us (3%)
    psum x1, waiting for transfers between devices, from_root(): return lax.psum(block, axis)  294 us
    another operation x3, other arithmetic  35.1 us
    psum x1, waiting for transfers between devices, chi_block(): summed = lax.psum(local, 'grid')  34.7 us
    all_gather x1, waiting for transfers between devices, chi_block(): gathered = lax.all_gather(summed, 'band', axis=0, tiled=True)  25.2 us
    convert_element_type x2, other arithmetic, planes_of(): val_bands = from_root(valence, 'band', owners[round_no]).astype(jnp.float32)  24.8 us
    dot_general x2, matrix products, planes_of(): jnp.einsum('bxyk,kq->bxyq', density, wide, preferred_element_type=jnp.flo...  14.5 us
    select_n x1, other arithmetic, from_root(): jnp.where(lax.axis_index(axis) == owner, block, jnp.zeros_like(block))  14.2 us
    mul x1, local copies, waits for them, and re-layouts, planes_of(): dens_re = val_bands[:, 0] * cond_f[0] + val_bands[:, 1] * cond_f[1]  11.5 us
  transfers between devices with their start and end apart: 3, of which 3 were waited for; matrix products, arithmetic and copies ran while one was open for 5% of the time, Pallas kernels for 0%

profile of v1, /device:TPU:0, one launch (start us, length us, event | category | flops | bytes accessed | tf_op | source)
XLA Modules:
  0.0 513.5 jit_solution(15172837455862605123)
XLA Ops:
  6.5 1.3 fusion.74
  9.2 14.2 %broadcast_select_fusion.1 = (bf16[2,2,40,160,160]{4,3,2,0,1:T(8,128)(2,1)}, bf16[2,2,40,160,160]{4,3,2,0,1:T(8,128)(2,1)}) fusion(pred[]{:T(512)S(6)} %eq.49, bf16[2,2,40,160,160]{4,3,2,1,0:T(8,128)(2,1)} %param.7, pred[]{:T(512)S(6)} %eq.50), kind=kLoop, calls=%fused_computation.9 | loop fusion | flops 8192000 | bytes 24576002 | tf_op jit(solution)/shard_map/jit(_where)/select_n | solution.py:14
  23.5 10.3 %convert_element_type.99 = f32[1,2,40,160,160]{4,3,2,1,0:T(8,128)} convert(bf16[1,2,40,160,160]{4,3,2,1,0:T(8,128)(2,1)} %param.8) | non-fusion elementwise | flops 2048000 | bytes 12288000 | tf_op jit(solution)/shard_map/convert_element_type | solution.py:40
  36.5 11.5 %slice_bitcast_fusion.5 = (f32[40,160,160]{2,1,0:T(8,128)}, f32[40,160,160]{2,1,0:T(8,128)}) fusion(f32[1,2,40,160,160]{4,3,2,1,0:T(8,128)} %convert_element_type.99), kind=kLoop, calls=%fused_computation.22 | loop fusion | bytes 16384000 | tf_op jit(solution)/shard_map/mul | solution.py:44
  48.2 2.7 fusion.27
  50.9 294.5 %all-reduce.6.cloned.1.call-done = (bf16[2,2,40,160,160]{4,3,2,0,1:T(8,128)(2,1)}, bf16[2,2,40,160,160]{4,3,2,0,1:T(8,128)(2,1)}) async-done(((bf16[2,2,40,160,160]{4,3,2,0,1:T(8,128)(2,1)}, bf16[2,2,40,160,160]{4,3,2,0,1:T(8,128)(2,1)}), (bf16[2,2,40,160,160]{4,3,2,0,1:T(8,128)(2,1)}, bf16[2,2,40,160,160]{4,3,2,0,1:T(8,128)(2,1)})) %all-reduce.6.cloned.1.call-update) | async-done | bytes 16384016 | tf_op jit(solution)/shard_map/psum | solution.py:15
  345.4 15.7 %convert_element_type.102 = f32[2,2,40,160,160]{4,3,2,0,1:T(8,128)} convert(bf16[2,2,40,160,160]{4,3,2,0,1:T(8,128)(2,1)} %get-tuple-element.7) | non-fusion elementwise | flops 4096000 | bytes 24576000 | tf_op jit(solution)/shard_map/convert_element_type | solution.py:43
  361.0 2.5 copy-done
  363.5 9.2 %convert_element_type.98 = f32[2,2,40,160,160]{4,3,2,0,1:T(8,128)} convert(bf16[2,2,40,160,160]{4,3,2,0,1:T(8,128)(2,1)S(1)} %copy-done) | non-fusion elementwise | flops 4096000 | bytes 24576000 | tf_op jit(solution)/shard_map/convert_element_type | solution.py:43
  372.7 32.0 %add_convert_fusion.1 = (bf16[2,40,160,160]{3,2,1,0:T(8,128)(2,1)}, bf16[2,40,160,160]{3,2,1,0:T(8,128)(2,1)}, bf16[2,40,160,160]{3,2,1,0:T(8,128)(2,1)}, bf16[2,40,160,160]{3,2,1,0:T(8,128)(2,1)}) fusion(f32[2,2,40,160,160]{4,3,2,0,1:T(8,128)} %convert_element_type.98, f32[40,160,160]{2,1,0:T(8,128)} %get-tuple-element.16, ...), kind=kLoop, calls=%fused_computation.7 | loop fusion | flops 32768000 | bytes 57344000 | tf_op jit(solution)/shard_map/convert.10
  404.7 8.6 %fusion.15 = bf16[2,40,160,42]{2,3,1,0:T(8,128)(2,1)S(1)} fusion(bf16[2,40,160,160]{3,2,1,0:T(8,128)(2,1)} %get-tuple-element.10, bf16[2,40,160,160]{3,2,1,0:T(8,128)(2,1)} %get-tuple-element.9, bf16[160,21]{0,1:T(8,128)(2,1)S(1)} %get-tuple-element.32, bf16[160,21]{0,1:T(8,128)(2,1)S(1)} %get-tuple-element.31, bf16[160,21]{0,1:T(8,128)(2,1)S(1)} %fusion.53), kind=kOutput, calls=%fused_computation.30 | convolution fusion | flops 361093120 | bytes 9287360 | tf_op jit(solution)/shard_map/bxyk,kq->bxyq/dot_general | solution.py:47
  413.3 1.1 convolution_bitcast_fusion.5
  414.4 1.2 convolution_bitcast_fusion.4
  415.6 5.9 %fusion.12 = bf16[2,40,160,42]{2,3,1,0:T(8,128)(2,1)S(1)} fusion(bf16[2,40,160,160]{3,2,1,0:T(8,128)(2,1)S(1)} %copy-done.1, bf16[2,40,160,160]{3,2,1,0:T(8,128)(2,1)S(1)} %copy-done.2, bf16[160,21]{0,1:T(8,128)(2,1)S(1)} %get-tuple-element.32, bf16[160,21]{0,1:T(8,128)(2,1)S(1)} %get-tuple-element.31, bf16[160,21]{0,1:T(8,128)(2,1)S(1)} %fusion.53), kind=kOutput, calls=%fused_computation.29 | convolution fusion | flops 361093120 | bytes 9287360 | tf_op jit(solution)/shard_map/bxyk,kq->bxyq/dot_general | solution.py:47
  421.5 1.1 convolution_bitcast_fusion.3
  422.6 1.2 convolution_bitcast_fusion.2
  423.8 1.6 fusion.21
  425.3 1.4 copy.40
  427.5 1.4 copy.41
  429.7 1.5 fusion.19
  431.3 1.4 copy.45
  432.8 1.4 copy.46
  434.4 1.8 fusion.9
  436.2 1.0 add_reduce_fusion
  437.4 0.8 maximum_multiply_fusion
  438.2 34.7 %all-reduce.4.cloned.1.call-done = f32[4,2,4096]{2,1,0:T(2,128)} async-done(((f32[4,2,4096]{2,1,0:T(2,128)}), f32[4,2,4096]{2,1,0:T(2,128)}) %all-reduce.4.cloned.1.call-update) | async-done | bytes 131088 | tf_op jit(solution)/shard_map/psum | solution.py:76
  472.9 25.2 %all-gather.2.cloned.1.call-done = f32[32,2,4096]{2,1,0:T(2,128)} async-done(((f32[4,2,4096]{2,1,0:T(2,128)}), f32[32,2,4096]{2,1,0:T(2,128)}) %all-gather.2.cloned.1.call-update) | async-done | bytes 1048592 | tf_op jit(solution)/shard_map/all_gather | solution.py:77
  498.1 1.4 dynamic-slice_negate_fusion
  499.6 1.2 constant_dynamic-slice_fusion
  500.8 1.8 convolution_bitcast_fusion.1
  502.7 1.8 convolution_bitcast_fusion
  504.5 2.5 pad_maximum_fusion
  (43 shorter events, 4.4 us)
Async XLA Ops:
  6.5 338.8 %all-reduce.6.cloned.1.call-start = ((), (), s32[]{:S(2)}) async-start(), calls=%async_computation.2 | async-start | bytes 52428800 | tf_op jit(solution)/shard_map/psum | solution.py:15
  23.4 10.4 %copy-start.6 = (s32[2]{0:T(128)S(1)}, s32[2]{0:T(128)}, u32[]{:S(2)}) copy-start(s32[2]{0:T(128)} %param.12) | copy-start | bytes 28
  23.4 11.2 %copy-start.7 = (f32[8]{0:T(128)S(1)}, f32[8]{0:T(128)}, u32[]{:S(2)}) copy-start(f32[8]{0:T(128)} %param.10) | copy-start | bytes 100
  23.4 11.9 %copy-start.8 = (f32[16]{0:T(128)S(1)}, f32[16]{0:T(128)}, u32[]{:S(2)}) copy-start(f32[16]{0:T(128)} %param.9) | copy-start | bytes 196
  23.4 449.5 %all-reduce.4.cloned.1.call-start = ((), (), s32[]{:S(2)}) async-start(), calls=%async_computation | async-start | bytes 262144 | tf_op jit(solution)/shard_map/psum | solution.py:76
  36.5 11.5 %copy-start.5 = (s32[3,4096]{1,0:T(4,128)S(1)}, s32[3,4096]{1,0:T(4,128)}, u32[]{:S(2)}) copy-start(s32[3,4096]{1,0:T(4,128)} %param.13) | copy-start | bytes 147460
  345.4 18.1 %copy-start = (bf16[2,2,40,160,160]{4,3,2,0,1:T(8,128)(2,1)S(1)}, bf16[2,2,40,160,160]{4,3,2,0,1:T(8,128)(2,1)}, u32[]{:S(2)}) copy-start(bf16[2,2,40,160,160]{4,3,2,0,1:T(8,128)(2,1)} %get-tuple-element.8) | copy-start | bytes 24576004
  404.6 10.9 %copy-start.1 = (bf16[2,40,160,160]{3,2,1,0:T(8,128)(2,1)S(1)}, bf16[2,40,160,160]{3,2,1,0:T(8,128)(2,1)}, u32[]{:S(2)}) copy-start(bf16[2,40,160,160]{3,2,1,0:T(8,128)(2,1)} %get-tuple-element.13) | copy-start | bytes 12288004
  404.6 11.0 %copy-start.2 = (bf16[2,40,160,160]{3,2,1,0:T(8,128)(2,1)S(1)}, bf16[2,40,160,160]{3,2,1,0:T(8,128)(2,1)}, u32[]{:S(2)}) copy-start(bf16[2,40,160,160]{3,2,1,0:T(8,128)(2,1)} %get-tuple-element.14) | copy-start | bytes 12288004
  429.7 4.7 copy-start.3
  429.7 4.7 copy-start.4
  438.2 60.0 %all-gather.2.cloned.1.call-start = ((), (), s32[]{:S(2)}) async-start(), calls=%async_computation.1 | async-start | bytes 1179648 | tf_op jit(solution)/shard_map/all_gather | solution.py:77
Sparse Core Ops, SparseCore 0:
  23.5 321.8 all-reduce.5
  438.3 34.5 all-reduce.3
  475.0 23.1 all-gather.1

commit v2 on v1

--- a/solution.py
+++ b/solution.py
@@ -1,18 +1,17 @@
+import functools
 import math
 
 import jax
 import jax.numpy as jnp
+import numpy as np
 from jax import lax
+from jax.experimental import pallas as pl
+from jax.experimental.pallas import tpu as pltpu
 from jax.sharding import PartitionSpec as P
 
 ROUNDS = 2
 GMAX = 10
 SIDE = 2 * GMAX + 1
-
-
-def from_root(block, axis, owner):
-    block = jnp.where(lax.axis_index(axis) == owner, block, jnp.zeros_like(block))
-    return lax.psum(block, axis)
 
 
 def twiddles(freqs, positions, length):
@@ -21,39 +20,226 @@
     return jnp.cos(angles).astype(jnp.bfloat16), jnp.sin(angles).astype(jnp.bfloat16)
 
 
-def low_tables(length):
-    freqs = (jnp.arange(SIDE, dtype=jnp.int32) - GMAX) % length
-    return twiddles(freqs[None, :], jnp.arange(length, dtype=jnp.int32)[:, None], length)
+MESH = pl.DeviceIdType.MESH
+LANES = 128
+PACK = 4
+KPAD = 32
+ROWS = 32
+
+
+def low_numpy(length):
+    freqs = np.arange(SIDE) - GMAX
+    angles = (np.arange(length)[:, None] * freqs[None, :]) % length * (2.0 * math.pi / length)
+    pad = ((0, 0), (0, KPAD - SIDE))
+    return np.pad(np.cos(angles), pad), np.pad(np.sin(angles), pad)
+
+
+def z_table(length):
+    cos_low, sin_low = low_numpy(length)
+    tail = length - LANES
+
+    def spread(table):
+        out = np.zeros((PACK + 1, LANES, PACK, KPAD))
+        for i in range(PACK):
+            out[i, :, i] = table[:LANES]
+            out[PACK, i * tail : (i + 1) * tail, i] = table[LANES:]
+        return out.reshape(PACK + 1, LANES, PACK * KPAD)
+
+    cos_wide, sin_wide = spread(cos_low), spread(sin_low)
+    top = np.concatenate([cos_wide, -sin_wide], axis=2)
+    low = np.concatenate([sin_wide, cos_wide], axis=2)
+    return jnp.asarray(np.concatenate([top, low], axis=1), jnp.float32).astype(jnp.bfloat16)
+
+
+def y_table(length):
+    cos_low, sin_low = low_numpy(length)
+    return jnp.asarray(np.concatenate([cos_low, sin_low], axis=1).T, jnp.float32).astype(jnp.bfloat16)
+
+
+def pack_kernel(in_ref, out_ref):
+    bands = in_ref.shape[0]
+    length = in_ref.shape[3]
+    for band in range(bands):
+        for comp in range(2):
+            tails = []
+            for i in range(PACK):
+                whole = in_ref[band, comp, i]
+                for block in range(length // ROWS):
+                    out_ref[band, block, comp, i] = whole[block * ROWS : (block + 1) * ROWS, :LANES]
+                tails.append(whole[:, LANES:])
+            tail = jnp.concatenate(tails, axis=1)
+            for block in range(length // ROWS):
+                out_ref[band, block, comp, PACK] = tail[block * ROWS : (block + 1) * ROWS]
+
+
+def packed(wave):
+    bands, _, x_local, length, _ = wave.shape
+    blocks = length // ROWS
+    groups = x_local // PACK
+    return pl.pallas_call(
+        pack_kernel,
+        grid=(groups,),
+        out_shape=jax.ShapeDtypeStruct(
+            (bands, groups * blocks, 2, PACK + 1, ROWS, LANES), jnp.bfloat16
+        ),
+        in_specs=[pl.BlockSpec((bands, 2, PACK, length, length), lambda g: (0, 0, g, 0, 0))],
+        out_specs=pl.BlockSpec(
+            (bands, blocks, 2, PACK + 1, ROWS, LANES), lambda g: (0, g, 0, 0, 0, 0)
+        ),
+        compiler_params=pltpu.CompilerParams(vmem_limit_bytes=32 * 2**20),
+    )(wave)
+
+
+def to_gray(position, bits):
+    index = 0
+    for bit in range(bits):
+        here = position // 2**bit % 2
+        above = position // 2 ** (bit + 1) % 2
+        index = index + (here + above) % 2 * 2**bit
+    return index
+
+
+def from_gray(index, bits):
+    position = 0
+    last = 0
+    for bit in reversed(range(bits)):
+        last = (last + index // 2**bit % 2) % 2
+        position = position + last * 2**bit
+    return position
+
+
+def ring_kernel(
+    count, info_ref, val_ref, cond_ref, wz_ref, wy_ref, out_ref, buf, along_z, send_sem, recv_sem
+):
+    bits = count.bit_length() - 1
+    slots = count + 1
+    chunks = val_ref.shape[1]
+    me = lax.axis_index("band")
+    position = from_gray(me, bits)
+    after = to_gray((position + 1) % count, bits)
+    before = to_gray((position + count - 1) % count, bits)
+    targets = (after, before)
+    starts = (position, count - 1 - position)
+    last = chunks + count - 2
+
+    barrier = pltpu.get_barrier_semaphore()
+    for neighbour in targets:
+        pl.semaphore_signal(barrier, inc=1, device_id={"band": neighbour}, device_id_type=MESH)
+    pl.semaphore_wait(barrier, 2)
+
+    streams = [(r, d) for r in range(ROUNDS) for d in range(2)]
+
+    def copy_of(stream, step):
+        now, later = step % slots, (step + 1) % slots
+        return pltpu.make_async_remote_copy(
+            src_ref=buf.at[stream, now],
+            dst_ref=buf.at[stream, later],
+            send_sem=send_sem.at[stream, step % 2],
+            recv_sem=recv_sem.at[stream, later],
+            device_id={"band": targets[stream % 2]},
+            device_id_type=MESH,
+        )
+
+    def step_body(step, carry):
+        now = step % slots
+        chunk = [(step + chunks - start) % chunks for start in starts]
+        for stream, (r, d) in enumerate(streams):
+            @pl.when(step > 0)
+            def _():
+                copy_of(stream, step + slots - 1).wait_recv()
+
+            own = jnp.logical_or(info_ref[stream] == 1, step == 0)
+            buf[stream, now] = jnp.where(own, val_ref[d, chunk[d]], buf[stream, now])
+
+            @pl.when(step < last)
+            def _():
+                copy_of(stream, step).start()
+
+        for stream in range(len(streams)):
+            @pl.when(step > 0)
+            def _():
+                copy_of(stream, step - 1).wait_send()
+
+        @pl.when(step >= count - 1)
+        def _():
+            held = [(chunk[d] + info_ref[len(streams) + i]) % chunks for i, (r, d) in enumerate(streams)]
+            cond = [cond_ref[0, index].astype(jnp.float32) for index in held]
+            total = None
+            for j in range(PACK + 1):
+                parts = []
+                for stream, (r, d) in enumerate(streams):
+                    v_re = buf[stream, now, 0, j].astype(jnp.float32)
+                    v_im = buf[stream, now, 1, j].astype(jnp.float32)
+                    c_re, c_im = cond[stream][0, j], cond[stream][1, j]
+                    d_re = (v_re * c_re + v_im * c_im).astype(jnp.bfloat16)
+                    d_im = (v_re * c_im - v_im * c_re).astype(jnp.bfloat16)
+                    parts.append(jnp.concatenate([d_re, d_im], axis=1))
+                term = jnp.dot(
+                    jnp.concatenate(parts, axis=0), wz_ref[j], preferred_element_type=jnp.float32
+                )
+                total = term if total is None else total + term
+            rounded = total.astype(jnp.bfloat16)
+            for stream, (r, d) in enumerate(streams):
+                along_z[stream, chunk[d]] = rounded[stream * ROWS : (stream + 1) * ROWS]
+
+        return carry
+
+    lax.fori_loop(0, last + 1, step_body, 0)
+
+    groups = out_ref.shape[1]
+    blocks = chunks // groups
+
+    def group_body(group, carry):
+        for stream in range(len(streams)):
+            first = group * blocks + chunks - info_ref[len(streams) + stream]
+            block = jnp.concatenate(
+                [along_z[stream, (first + b) % chunks] for b in range(blocks)], axis=0
+            )
+            both = jnp.dot(wy_ref[...], block, preferred_element_type=jnp.float32)
+            cos_part, sin_part = both[:KPAD], both[KPAD:]
+            real = cos_part[:, :LANES] + sin_part[:, LANES:]
+            imag = cos_part[:, LANES:] - sin_part[:, :LANES]
+            out_ref[stream, group, 0] = real.astype(jnp.bfloat16)
+            out_ref[stream, group, 1] = imag.astype(jnp.bfloat16)
+        return carry
+
+    lax.fori_loop(0, groups, group_body, 0)
 
 
 def planes_of(valence, conduction, owners):
-    length = valence.shape[3]
-    val_dev, x_local = valence.shape[0], valence.shape[2]
-    cos_low, sin_low = low_tables(length)
-    wide = jnp.concatenate(
-        [
-            jnp.concatenate([cos_low, -sin_low], axis=1),
-            jnp.concatenate([sin_low, cos_low], axis=1),
+    val_dev, _, x_local, length, _ = valence.shape
+    groups = x_local // PACK
+    count = lax.axis_size("band")
+    streams = ROUNDS * val_dev
+    chunk = (2, PACK + 1, ROWS, LANES)
+    vmem = pl.BlockSpec(memory_space=pltpu.VMEM)
+    chunks = groups * (length // ROWS)
+    bits = count.bit_length() - 1
+    me = lax.axis_index("band")
+    behind = from_gray(me, bits) - from_gray(owners, bits)
+    shift = jnp.where(jnp.stack([behind < 0, behind > 0], axis=1), chunks - count, 0)
+    is_owner = jnp.broadcast_to((owners == me)[:, None], (ROUNDS, val_dev))
+    info = jnp.concatenate([is_owner.reshape(-1).astype(jnp.int32), shift.reshape(-1).astype(jnp.int32)])
+    plane = pl.pallas_call(
+        functools.partial(ring_kernel, count),
+        out_shape=jax.ShapeDtypeStruct((streams, groups, 2, KPAD, LANES), jnp.bfloat16),
+        in_specs=[pl.BlockSpec(memory_space=pltpu.SMEM), vmem, vmem, vmem, vmem],
+        out_specs=vmem,
+        scratch_shapes=[
+            pltpu.VMEM((streams, count + 1) + chunk, jnp.bfloat16),
+            pltpu.VMEM((streams, chunks, ROWS, 2 * LANES), jnp.bfloat16),
+            pltpu.SemaphoreType.DMA((streams, 2)),
+            pltpu.SemaphoreType.DMA((streams, count + 1)),
         ],
-        axis=0,
-    )
-    cond_f = conduction[0].astype(jnp.float32)
-    planes = []
-    for round_no in range(ROUNDS):
-        val_bands = from_root(valence, "band", owners[round_no]).astype(jnp.float32)
-        dens_re = val_bands[:, 0] * cond_f[0] + val_bands[:, 1] * cond_f[1]
-        dens_im = val_bands[:, 0] * cond_f[1] - val_bands[:, 1] * cond_f[0]
-        density = jnp.concatenate([dens_re, dens_im], axis=-1).astype(jnp.bfloat16)
-        along_z = jnp.einsum(
-            "bxyk,kq->bxyq", density, wide, preferred_element_type=jnp.float32
-        ).astype(jnp.bfloat16)
-        cos_part = jnp.einsum("bxyk,yq->bxqk", along_z, cos_low, preferred_element_type=jnp.float32)
-        sin_part = jnp.einsum("bxyk,yq->bxqk", along_z, sin_low, preferred_element_type=jnp.float32)
-        real_part = cos_part[..., :SIDE] + sin_part[..., SIDE:]
-        imag_part = cos_part[..., SIDE:] - sin_part[..., :SIDE]
-        plane = jnp.stack([real_part, imag_part], axis=1).astype(jnp.bfloat16)
-        planes.append(plane.reshape(val_dev, 2, x_local, SIDE * SIDE))
-    return jnp.concatenate(planes, axis=0)
+        compiler_params=pltpu.CompilerParams(
+            collective_id=0, has_side_effects=True, vmem_limit_bytes=48 * 2**20
+        ),
+        cost_estimate=pl.CostEstimate(
+            flops=streams * chunks * ROWS * 1280 * 512, bytes_accessed=2 * valence.size, transcendentals=0
+        ),
+    )(info, packed(valence), packed(conduction), z_table(length), y_table(length))
+    plane = plane.reshape(streams, groups, 2, KPAD, PACK, KPAD)[:, :, :, :SIDE, :, :SIDE]
+    return plane.transpose(0, 2, 1, 4, 3, 5).reshape(streams, 2, x_local, SIDE * SIDE)
 
 
 def chi_block(plane, gvectors, scale, length):

time: 514 us -> 278 us (0.54)
  waiting for transfers between devices: 354 us -> 61.3 us
  Pallas kernels: 0 us -> 175 us
  other arithmetic: 94.8 us -> 11.4 us
  matrix products: 24.6 us -> 5.37 us
  local copies, waits for them, and re-layouts: 24.3 us -> 10.9 us
    psum x1 -> x0, waiting for transfers between devices: 294 us -> none  [from_root(): return lax.psum(block, axis)]
    pallas_call x0 -> x3, Pallas kernels: none -> 175 us  [the longest x1 169 us: planes_of(): pl.pallas_call(functools.partial(ring_kernel, count), out_shape=jax.Shape...]
    convert_element_type x4 -> x0, other arithmetic: 35.3 us -> none  [the longest x2 24.8 us: planes_of(): val_bands = from_root(valence, 'band', owners[round_no]).astype(jnp.float32)]
    another operation x3 -> x2, other arithmetic: 35.1 us -> 0.7 us  [planes_of(): jnp.stack([behind < 0, behind > 0], axis=1)]
    dot_general x6 -> x0, matrix products: 19.1 us -> none  [the longest x2 14.5 us: planes_of(): jnp.einsum('bxyk,kq->bxyq', density, wide, preferred_element_type=jnp.flo...]
    select_n x2 -> x1, other arithmetic: 14.2 us -> 0.01 us  [planes_of(): jnp.where(jnp.stack([behind < 0, behind > 0], axis=1), chunks - count, 0)]
    mul x1 -> x0, local copies, waits for them, and re-layouts: 11.5 us -> none  [planes_of(): dens_re = val_bands[:, 0] * cond_f[0] + val_bands[:, 1] * cond_f[1]]
    another operation x8 -> x0, local copies, waits for them, and re-layouts: 7.52 us -> none
  transfers between devices with their start and end apart: 3 -> 2, of which waited for: 3 -> 2; matrix products, arithmetic and copies ran while one was open for 5% -> 0% of each run, Pallas kernels for 0% -> 0%
where the time goes in v2:
time: 278 us
  Pallas kernels  175 us (63%)
  waiting for transfers between devices  61.3 us (22%)
  between operations  14.3 us (5%)
  other arithmetic  11.4 us (4%)
  local copies, waits for them, and re-layouts  10.9 us (4%)
  matrix products  5.37 us (2%)
    pallas_call x1, Pallas kernels, planes_of(): pl.pallas_call(functools.partial(ring_kernel, count), out_shape=jax.Shape...  169 us
    psum x1, waiting for transfers between devices, chi_block(): summed = lax.psum(local, 'grid')  36.1 us
    all_gather x1, waiting for transfers between devices, chi_block(): gathered = lax.all_gather(summed, 'band', axis=0, tiled=True)  25.2 us
    unnamed x17, local copies, waits for them, and re-layouts  6.22 us
    pallas_call x2, Pallas kernels, packed(): pl.pallas_call(pack_kernel, grid=(groups,), out_shape=jax.ShapeDtypeStruc...  6.07 us
  transfers between devices with their start and end apart: 2, of which 2 were waited for; matrix products, arithmetic and copies ran while one was open for 0% of the time, Pallas kernels for 0%

profile of v2, /device:TPU:0, one launch (start us, length us, event | category | flops | bytes accessed | tf_op | source)
XLA Modules:
  0.0 278.2 jit_solution(5328800032983537241)
XLA Ops:
  6.5 0.7 broadcast_multiply_fusion
  7.2 0.7 compare_bitcast_fusion.1
  7.9 0.1 copy.21
  8.0 0.1 select_n.134
  8.2 0.1 convert_element_type.53
  8.3 4.7 %copy-done = bf16[2,2,40,160,160]{4,3,2,1,0:T(8,128)(2,1)S(1)} copy-done((bf16[2,2,40,160,160]{4,3,2,1,0:T(8,128)(2,1)S(1)}, bf16[2,2,40,160,160]{4,3,2,1,0:T(8,128)(2,1)}, u32[]{:S(2)}) %copy-start) | copy-done | bytes 8192024
  13.0 4.0 %shard_map.91.val_ref = bf16[2,50,2,5,32,128]{5,4,3,2,1,0:T(8,128)(2,1)S(1)} custom-call(bf16[2,2,40,160,160]{4,3,2,1,0:T(8,128)(2,1)S(1)} %copy-done), custom_call_target="tpu_custom_call" | custom-call | tf_op jit(solution)/shard_map/pallas_call | solution.py:79
  17.0 2.1 shard_map.92.cond_ref
  19.1 1.1 copy-done.1
  20.2 0.1 pad_add_fusion.info_ref
  20.2 168.7 %shard_map.93 = bf16[4,10,2,32,128]{4,3,2,1,0:T(8,128)(2,1)S(1)} custom-call(s32[8]{0:T(128)S(1)} %pad_add_fusion.info_ref, bf16[2,50,2,5,32,128]{5,4,3,2,1,0:T(8,128)(2,1)} %copy-done.1, bf16[1,50,2,5,32,128]{5,4,3,2,1,0:T(8,128)(2,1)S(1)} %shard_map.92.cond_ref, bf16[5,256,256]{2,1,0:T(8,128)(2,1)S(1)} %copy-done.3, bf16[64,160]{1,0:T(8,128)(2,1)S(1)} %copy-done.4), custom_call_target="tpu_custom_call" | custom-call | flops 4194304000 | bytes 8192000 | tf_op jit(solution)/shard_map/pallas_call | solution.py:223
  188.9 1.1 reshape.114
  190.0 0.7 slice.47
  190.8 0.4 copy.40
  191.2 1.1 dot_general.11
  192.3 0.2 fusion.33
  192.4 1.7 fusion.1
  194.1 2.7 fusion.9
  196.9 1.0 add_reduce_fusion
  198.1 0.1 add.185
  198.8 0.2 select_reduce_fusion
  199.0 0.6 fusion.22
  199.6 0.6 sqrt_multiply_fusion
  200.2 0.8 maximum_multiply_fusion
  201.0 0.2 all-gather.2.cloned.1.call-start
  201.2 36.1 %all-reduce.2.cloned.1.call-done = f32[4,2,4096]{2,1,0:T(2,128)} async-done(((f32[4,2,4096]{2,1,0:T(2,128)}), f32[4,2,4096]{2,1,0:T(2,128)}) %all-reduce.2.cloned.1.call-update) | async-done | bytes 131088 | tf_op jit(solution)/shard_map/psum | solution.py:262
  237.3 25.2 %all-gather.2.cloned.1.call-done = f32[32,2,4096]{2,1,0:T(2,128)} async-done(((f32[4,2,4096]{2,1,0:T(2,128)}), f32[32,2,4096]{2,1,0:T(2,128)}) %all-gather.2.cloned.1.call-update) | async-done | bytes 1048592 | tf_op jit(solution)/shard_map/all_gather | solution.py:263
  262.5 1.4 dynamic-slice_negate_fusion
  264.0 1.2 constant_dynamic-slice_fusion
  265.2 1.8 convolution_bitcast_fusion.1
  267.1 1.8 convolution_bitcast_fusion
  268.9 2.5 pad_maximum_fusion
  (27 shorter events, 0.4 us)
Async XLA Ops:
  6.5 230.8 %all-reduce.2.cloned.1.call-start = ((), (), s32[]{:S(2)}) async-start(), calls=%async_computation | async-start | bytes 262144 | tf_op jit(solution)/shard_map/psum | solution.py:262
  8.3 4.7 %copy-start = (bf16[2,2,40,160,160]{4,3,2,1,0:T(8,128)(2,1)S(1)}, bf16[2,2,40,160,160]{4,3,2,1,0:T(8,128)(2,1)}, u32[]{:S(2)}) copy-start(bf16[2,2,40,160,160]{4,3,2,1,0:T(8,128)(2,1)} %in_ref.2) | copy-start | bytes 24576004
  13.0 4.0 %copy-start.2 = (bf16[1,2,40,160,160]{4,3,2,1,0:T(8,128)(2,1)S(1)}, bf16[1,2,40,160,160]{4,3,2,1,0:T(8,128)(2,1)}, u32[]{:S(2)}) copy-start(bf16[1,2,40,160,160]{4,3,2,1,0:T(8,128)(2,1)} %in_ref.3) | copy-start | bytes 12288004
  17.0 3.2 %copy-start.1 = (bf16[2,50,2,5,32,128]{5,4,3,2,1,0:T(8,128)(2,1)}, bf16[2,50,2,5,32,128]{5,4,3,2,1,0:T(8,128)(2,1)S(1)}, u32[]{:S(2)}) copy-start(bf16[2,50,2,5,32,128]{5,4,3,2,1,0:T(8,128)(2,1)S(1)} %shard_map.91.val_ref) | copy-start | bytes 24576004
  17.0 3.2 %copy-start.3 = (bf16[5,256,256]{2,1,0:T(8,128)(2,1)S(1)}, bf16[5,256,256]{2,1,0:T(8,128)(2,1)}, u32[]{:S(2)}) copy-start(bf16[5,256,256]{2,1,0:T(8,128)(2,1)} %constant.187.wz_ref) | copy-start | bytes 1966084
  17.0 3.2 %copy-start.4 = (bf16[64,160]{1,0:T(8,128)(2,1)S(1)}, bf16[64,160]{1,0:T(8,128)(2,1)}, u32[]{:S(2)}) copy-start(bf16[64,160]{1,0:T(8,128)(2,1)} %constant.188.wy_ref) | copy-start | bytes 61444
  190.8 1.5 copy-start.5
  196.8 2.0 copy-start.6
  196.9 2.1 copy-start.7
  201.0 61.5 %all-gather.2.cloned.1.call-start = ((), (), s32[]{:S(2)}) async-start(), calls=%async_computation.1 | async-start | bytes 1179648 | tf_op jit(solution)/shard_map/all_gather | solution.py:263
Sparse Core Ops, SparseCore 0:
  201.1 36.1 all-reduce.1
  239.3 23.1 all-gather.1

commit v3 on v2

--- a/solution.py
+++ b/solution.py
@@ -24,7 +24,7 @@
 LANES = 128
 PACK = 4
 KPAD = 32
-ROWS = 32
+ROWS = 80
 
 
 def low_numpy(length):
@@ -242,9 +242,153 @@
     return plane.transpose(0, 2, 1, 4, 3, 5).reshape(streams, 2, x_local, SIDE * SIDE)
 
 
+def spread_kernel(
+    bands, grids, local_ref, rows_ref, cols_ref, parts, total, part_send, part_recv, row_send, row_recv, col_send, col_recv
+):
+    band = lax.axis_index("band")
+    grid = lax.axis_index("grid")
+    ratio = bands // grids
+    col_count = cols_ref.shape[2]
+    source = band // ratio
+    in_own = source == grid
+
+    barrier = pltpu.get_barrier_semaphore()
+
+    def greet(to_band, to_grid):
+        pl.semaphore_signal(
+            barrier, inc=1, device_id={"band": to_band, "grid": to_grid}, device_id_type=MESH
+        )
+
+    for j in range(1, grids):
+        greet(band, (grid + j) % grids)
+    for j in range(1, bands):
+        greet((band + j) % bands, grid)
+    for b in range(bands):
+        @pl.when(jnp.logical_not(jnp.logical_and(in_own, b == band)))
+        def _():
+            greet(b, source)
+    pl.semaphore_wait(
+        barrier, grids - 1 + bands - 1 + bands - jnp.where(in_own, 1, 0).astype(jnp.int32)
+    )
+
+    def part_copy(j):
+        peer = (grid + j) % grids
+        return pltpu.make_async_remote_copy(
+            src_ref=local_ref.at[peer],
+            dst_ref=parts.at[j],
+            send_sem=part_send.at[j],
+            recv_sem=part_recv.at[j],
+            device_id={"band": band, "grid": peer},
+            device_id_type=MESH,
+        )
+
+    def row_copy(j):
+        return pltpu.make_async_remote_copy(
+            src_ref=total,
+            dst_ref=rows_ref.at[band],
+            send_sem=row_send.at[j],
+            recv_sem=row_recv.at[j],
+            device_id={"band": (band + j) % bands, "grid": grid},
+            device_id_type=MESH,
+        )
+
+    def col_copy(q, g):
+        return pltpu.make_async_remote_copy(
+            src_ref=total.at[:, pl.ds(q * col_count, col_count)],
+            dst_ref=cols_ref.at[band],
+            send_sem=col_send.at[q * grids + g],
+            recv_sem=col_recv.at[band],
+            device_id={"band": grid * ratio + q, "grid": g},
+            device_id_type=MESH,
+        )
+
+    def is_me(q, g):
+        return jnp.logical_and(grid * ratio + q == band, grid == g)
+
+    for j in range(1, grids):
+        part_copy(j).start()
+    summed = local_ref[grid]
+    for j in range(1, grids):
+        part_copy(j).wait_recv()
+        summed = summed + parts[j]
+    total[...] = summed
+    for q in range(ratio):
+        for g in range(grids):
+            @pl.when(jnp.logical_not(is_me(q, g)))
+            def _():
+                col_copy(q, g).start()
+    for j in range(1, bands):
+        row_copy(j).start()
+    rows_ref[band] = summed
+    for q in range(ratio):
+        @pl.when(is_me(q, grid))
+        def _():
+            cols_ref[band] = summed[:, q * col_count : (q + 1) * col_count]
+
+    for j in range(1, bands):
+        pltpu.make_async_remote_copy(
+            src_ref=total,
+            dst_ref=rows_ref.at[(band + bands - j) % bands],
+            send_sem=row_send.at[j],
+            recv_sem=row_recv.at[j],
+            device_id={"band": (band + j) % bands, "grid": grid},
+            device_id_type=MESH,
+        ).wait_recv()
+    for b in range(bands):
+        @pl.when(jnp.logical_not(jnp.logical_and(in_own, b == band)))
+        def _():
+            pltpu.make_async_remote_copy(
+                src_ref=total.at[:, pl.ds(0, col_count)],
+                dst_ref=cols_ref.at[b],
+                send_sem=col_send.at[0],
+                recv_sem=col_recv.at[b],
+                device_id={"band": b, "grid": source},
+                device_id_type=MESH,
+            ).wait_recv()
+    for j in range(1, grids):
+        part_copy(j).wait_send()
+    for j in range(1, bands):
+        row_copy(j).wait_send()
+    for q in range(ratio):
+        for g in range(grids):
+            @pl.when(jnp.logical_not(is_me(q, g)))
+            def _():
+                col_copy(q, g).wait_send()
+
+
+def spread(local):
+    bands, grids = lax.axis_size("band"), lax.axis_size("grid")
+    lines, count = local.shape
+    row_count, col_count = count // grids, count // bands
+    by_grid = local.reshape(lines, grids, row_count).transpose(1, 0, 2)
+    vmem = pl.BlockSpec(memory_space=pltpu.VMEM)
+    dma = pltpu.SemaphoreType.DMA
+    return pl.pallas_call(
+        functools.partial(spread_kernel, bands, grids),
+        out_shape=(
+            jax.ShapeDtypeStruct((bands, lines, row_count), jnp.float32),
+            jax.ShapeDtypeStruct((bands, lines, col_count), jnp.float32),
+        ),
+        in_specs=[vmem],
+        out_specs=(vmem, vmem),
+        scratch_shapes=[
+            pltpu.VMEM((grids, lines, row_count), jnp.float32),
+            pltpu.VMEM((lines, row_count), jnp.float32),
+            dma((grids,)),
+            dma((grids,)),
+            dma((bands,)),
+            dma((bands,)),
+            dma((bands,)),
+            dma((bands,)),
+        ],
+        compiler_params=pltpu.CompilerParams(
+            collective_id=1, has_side_effects=True, vmem_limit_bytes=32 * 2**20
+        ),
+    )(by_grid)
+
+
 def chi_block(plane, gvectors, scale, length):
     grid_pos = lax.axis_index("grid")
-    band_pos = lax.axis_index("band")
     pairs, _, x_local, _ = plane.shape
     freq_x, freq_y, freq_z = (gvectors[0], gvectors[1], gvectors[2])
     count = freq_x.shape[0]
@@ -259,12 +403,10 @@
     elem_re = jnp.sum(at_g[:, 0] * cos_g + at_g[:, 1] * sin_g, axis=1)
     elem_im = jnp.sum(at_g[:, 1] * cos_g - at_g[:, 0] * sin_g, axis=1)
     local = jnp.stack([elem_re, elem_im], axis=1) * scale[:, None, None]
-    summed = lax.psum(local, "grid")
-    gathered = lax.all_gather(summed, "band", axis=0, tiled=True)
-    row_count = count // lax.axis_size("grid")
-    col_count = count // lax.axis_size("band")
-    rows = lax.dynamic_slice_in_dim(gathered, grid_pos * row_count, row_count, 2)
-    cols = lax.dynamic_slice_in_dim(gathered, band_pos * col_count, col_count, 2)
+    bands = lax.axis_size("band")
+    rows, cols = spread(local.reshape(pairs * 2, count))
+    rows = rows.reshape(bands * pairs, 2, -1)
+    cols = cols.reshape(bands * pairs, 2, -1)
     right_side = jnp.concatenate([cols[:, 0], cols[:, 1]], axis=0)
     left_real = jnp.concatenate([-rows[:, 0], -rows[:, 1]], axis=0)
     left_imag = jnp.concatenate([-rows[:, 1], rows[:, 0]], axis=0)

time: 278 us -> 180 us (0.65)
  waiting for transfers between devices: 61.3 us -> 0 us
  Pallas kernels: 175 us -> 147 us
  between operations: 14.3 us -> 0.95 us
    pallas_call x1, Pallas kernels: 169 us -> 125 us  [planes_of(): pl.pallas_call(functools.partial(ring_kernel, count), out_shape=jax.Shape...]
    psum x1 -> x0, waiting for transfers between devices: 36.1 us -> none  [chi_block(): summed = lax.psum(local, 'grid')]
    all_gather x1 -> x0, waiting for transfers between devices: 25.2 us -> none  [chi_block(): gathered = lax.all_gather(summed, 'band', axis=0, tiled=True)]
    pallas_call x0 -> x1, Pallas kernels: none -> 15.6 us  [spread(): pl.pallas_call(functools.partial(spread_kernel, bands, grids), out_shape=...]
    unnamed x17 -> x19, local copies, waits for them, and re-layouts: 6.22 us -> 8.3 us
  transfers between devices with their start and end apart: 2 -> 0, of which waited for: 2 -> 0; matrix products, arithmetic and copies ran while one was open for 0% -> 0% of each run, Pallas kernels for 0% -> 0%
where the time goes in v3:
time: 180 us
  Pallas kernels  147 us (82%)
  local copies, waits for them, and re-layouts  12.4 us (7%)
  other arithmetic  11.8 us (7%)
  matrix products  7.69 us (4%)
    pallas_call x1, Pallas kernels, planes_of(): pl.pallas_call(functools.partial(ring_kernel, count), out_shape=jax.Shape...  125 us
    pallas_call x1, Pallas kernels, spread(): pl.pallas_call(functools.partial(spread_kernel, bands, grids), out_shape=...  15.6 us
    unnamed x19, local copies, waits for them, and re-layouts  8.3 us
    pallas_call x2, Pallas kernels, packed(): pl.pallas_call(pack_kernel, grid=(groups,), out_shape=jax.ShapeDtypeStruc...  6.06 us
    dot_general x1, matrix products, chi_block(): jnp.dot(plane.reshape(pairs * 2 * x_local, SIDE * SIDE), chosen, preferre...  4 us

profile of v3, /device:TPU:0, one launch (start us, length us, event | category | flops | bytes accessed | tf_op | source)
XLA Modules:
  0.0 179.6 jit_solution(18076217226147456040)
XLA Ops:
  0.0 0.7 compare_bitcast_fusion.1
  0.7 0.1 copy.21
  0.8 0.1 select_n.128
  1.0 0.1 convert_element_type.53
  1.1 4.7 %copy-done = bf16[2,2,40,160,160]{4,3,2,1,0:T(8,128)(2,1)S(1)} copy-done((bf16[2,2,40,160,160]{4,3,2,1,0:T(8,128)(2,1)S(1)}, bf16[2,2,40,160,160]{4,3,2,1,0:T(8,128)(2,1)}, u32[]{:S(2)}) %copy-start) | copy-done | bytes 8192024
  5.9 4.0 %shard_map.91.val_ref = bf16[2,20,2,5,80,128]{5,4,3,2,1,0:T(8,128)(2,1)S(1)} custom-call(bf16[2,2,40,160,160]{4,3,2,1,0:T(8,128)(2,1)S(1)} %copy-done), custom_call_target="tpu_custom_call" | custom-call | tf_op jit(solution)/shard_map/pallas_call | solution.py:79
  9.9 3.1 %copy-done.1 = bf16[2,20,2,5,80,128]{5,4,3,2,1,0:T(8,128)(2,1)} copy-done((bf16[2,20,2,5,80,128]{5,4,3,2,1,0:T(8,128)(2,1)}, bf16[2,20,2,5,80,128]{5,4,3,2,1,0:T(8,128)(2,1)S(1)}, u32[]{:S(2)}) %copy-start.1) | copy-done | bytes 8192024
  13.0 2.1 %shard_map.92.cond_ref = bf16[1,20,2,5,80,128]{5,4,3,2,1,0:T(8,128)(2,1)S(1)} custom-call(bf16[1,2,40,160,160]{4,3,2,1,0:T(8,128)(2,1)S(1)} %copy-done.2), custom_call_target="tpu_custom_call" | custom-call | tf_op jit(solution)/shard_map/pallas_call | solution.py:79
  15.1 125.2 %shard_map.93 = bf16[4,10,2,32,128]{4,3,2,1,0:T(8,128)(2,1)S(1)} custom-call(s32[8]{0:T(128)S(1)} %pad_add_fusion.info_ref, bf16[2,20,2,5,80,128]{5,4,3,2,1,0:T(8,128)(2,1)} %copy-done.1, bf16[1,20,2,5,80,128]{5,4,3,2,1,0:T(8,128)(2,1)S(1)} %shard_map.92.cond_ref, bf16[5,256,256]{2,1,0:T(8,128)(2,1)S(1)} %copy-done.3, bf16[64,160]{1,0:T(8,128)(2,1)S(1)} %copy-done.4), custom_call_target="tpu_custom_call" | custom-call | flops 4194304000 | bytes 8192000 | tf_op jit(solution)/shard_map/pallas_call | solution.py:223
  140.3 1.1 reshape.122
  141.4 0.7 slice.47
  142.1 0.4 copy.44
  142.5 1.1 dot_general.11
  143.6 0.2 fusion.35
  143.8 4.0 %fusion.1 = f32[4,2,40,4096]{3,2,1,0:T(8,128)} fusion(bf16[4,2,40,441]{3,2,1,0:T(8,128)(2,1)S(1)} %dot_general.11, s32[4096]{0:T(1024)S(1)} %bitcast.51), kind=kOutput, calls=%fused_computation.2 | convolution fusion | flops 1157861376 | bytes 5541504 | tf_op jit(solution)/shard_map/dot_general | solution.py:397
  147.8 2.7 %fusion.9 = (f32[40,4096]{1,0:T(8,128)S(1)}, f32[40,4096]{1,0:T(8,128)S(1)}) fusion(s32[40]{0:T(128)S(1)} %iota_add_fusion.1, s32[4096]{0:T(1024)S(1)} %bitcast.50), kind=kLoop, calls=%fused_computation.21 | loop fusion | flops 2129920 | bytes 1327264 | tf_op jit(solution)/shard_map/convert_element_type | solution.py:402
  150.5 3.6 %add_reduce_fusion = (f32[4,4096]{1,0:T(4,128)S(1)}, f32[4,4096]{1,0:T(4,128)S(1)}) fusion(f32[4,2,40,4096]{3,2,1,0:T(8,128)} %fusion.1, f32[40,4096]{1,0:T(8,128)S(1)} %get-tuple-element.20, f32[40,4096]{1,0:T(8,128)S(1)} %get-tuple-element.19), kind=kLoop, calls=%fused_computation.8 | loop fusion | flops 5210112 | bytes 6684672 | tf_op jit(solution)/shard_map/reduce_sum | solution.py:403
  154.2 0.1 pad_maximum_fusion.1
  154.3 0.1 stack.35
  154.6 0.1 add.177
  154.7 0.2 select_reduce_fusion
  155.5 0.7 fusion.23
  156.2 0.7 sqrt_multiply_fusion
  157.0 0.1 mul.136
  157.1 0.1 fusion.17.local_ref
  157.1 15.6 %shard_map.94 = (f32[8,8,1024]{2,1,0:T(8,128)S(1)}, f32[8,8,512]{2,1,0:T(8,128)S(1)}) custom-call(f32[4,8,1024]{2,1,0:T(8,128)S(1)} %fusion.17.local_ref), custom_call_target="tpu_custom_call" | custom-call | tf_op jit(solution)/shard_map/pallas_call | solution.py:366
  172.8 0.1 fusion.34
  172.9 0.1 reshape.123
  173.1 0.2 slice_negate_fusion
  173.4 1.8 %convolution_bitcast_fusion.1 = f32[1,1024,512]{2,1,0:T(8,128)S(1)} fusion(f32[32,1024]{1,0:T(8,128)S(1)} %get-tuple-element.23, f32[32,1024]{1,0:T(8,128)S(1)} %fusion.32, f32[32,512]{1,0:T(8,128)S(1)} %get-tuple-element.25, f32[32,512]{1,0:T(8,128)S(1)} %get-tuple-element.24), kind=kOutput, calls=%fused_computation.11 | convolution fusion | flops 402751488 | bytes 2490368 | tf_op jit(solution)/shard_map/pr,pc->rc/dot_general | solution.py:414
  175.3 1.8 %convolution_bitcast_fusion = f32[1,1024,512]{2,1,0:T(8,128)S(1)} fusion(f32[32,1024]{1,0:T(8,128)S(1)} %get-tuple-element.22, f32[32,1024]{1,0:T(8,128)S(1)} %get-tuple-element.23, f32[32,512]{1,0:T(8,128)S(1)} %get-tuple-element.25, f32[32,512]{1,0:T(8,128)S(1)} %get-tuple-element.24), kind=kOutput, calls=%fused_computation.10 | convolution fusion | flops 402751488 | bytes 2490368 | tf_op jit(solution)/shard_map/pr,pc->rc/dot_general | solution.py:415
  177.1 2.5 %pad_maximum_fusion = f32[2,1024,512]{2,1,0:T(8,128)} fusion(f32[1,1024,512]{2,1,0:T(8,128)S(1)} %convolution_bitcast_fusion, f32[1,1024,512]{2,1,0:T(8,128)S(1)} %convolution_bitcast_fusion.1), kind=kLoop, calls=%fused_computation.3 | loop fusion | flops 1048576 | bytes 8388608 | tf_op jit(solution)/shard_map/stack | solution.py:416
  (30 shorter events, 0.6 us)
Async XLA Ops:
  1.1 4.7 %copy-start = (bf16[2,2,40,160,160]{4,3,2,1,0:T(8,128)(2,1)S(1)}, bf16[2,2,40,160,160]{4,3,2,1,0:T(8,128)(2,1)}, u32[]{:S(2)}) copy-start(bf16[2,2,40,160,160]{4,3,2,1,0:T(8,128)(2,1)} %in_ref.2) | copy-start | bytes 24576004
  5.9 7.2 %copy-start.2 = (bf16[1,2,40,160,160]{4,3,2,1,0:T(8,128)(2,1)S(1)}, bf16[1,2,40,160,160]{4,3,2,1,0:T(8,128)(2,1)}, u32[]{:S(2)}) copy-start(bf16[1,2,40,160,160]{4,3,2,1,0:T(8,128)(2,1)} %in_ref.3) | copy-start | bytes 12288004
  9.9 3.2 %copy-start.1 = (bf16[2,20,2,5,80,128]{5,4,3,2,1,0:T(8,128)(2,1)}, bf16[2,20,2,5,80,128]{5,4,3,2,1,0:T(8,128)(2,1)S(1)}, u32[]{:S(2)}) copy-start(bf16[2,20,2,5,80,128]{5,4,3,2,1,0:T(8,128)(2,1)S(1)} %shard_map.91.val_ref) | copy-start | bytes 24576004
  13.0 2.1 %copy-start.3 = (bf16[5,256,256]{2,1,0:T(8,128)(2,1)S(1)}, bf16[5,256,256]{2,1,0:T(8,128)(2,1)}, u32[]{:S(2)}) copy-start(bf16[5,256,256]{2,1,0:T(8,128)(2,1)} %constant.181.wz_ref) | copy-start | bytes 1966084
  13.0 2.1 %copy-start.4 = (bf16[64,160]{1,0:T(8,128)(2,1)S(1)}, bf16[64,160]{1,0:T(8,128)(2,1)}, u32[]{:S(2)}) copy-start(bf16[64,160]{1,0:T(8,128)(2,1)} %constant.182.wy_ref) | copy-start | bytes 61444
  142.1 1.5 copy-start.5
  150.5 4.0 %copy-start.6 = (s32[2]{0:T(128)S(1)}, s32[2]{0:T(128)}, u32[]{:S(2)}) copy-start(s32[2]{0:T(128)} %param.14) | copy-start | bytes 28
  150.5 4.2 %copy-start.7 = (f32[16]{0:T(128)S(1)}, f32[16]{0:T(128)}, u32[]{:S(2)}) copy-start(f32[16]{0:T(128)} %param.11) | copy-start | bytes 196
  150.5 5.0 %copy-start.8 = (f32[8]{0:T(128)S(1)}, f32[8]{0:T(128)}, u32[]{:S(2)}) copy-start(f32[8]{0:T(128)} %param.12) | copy-start | bytes 100
